TPU v7x, 32 devices: a whole 2x2x4 slice. The times are simulated.
32 devices in a mesh: grp: 2 (over y), inp: 4 (over x, core), out: 4 (over z).
Axes of the slice: x: 2, y: 2, z: 4, core: 2. Of those that a mesh axis runs over, the one named last changes fastest.
Arguments:
- saved_inputs: bfloat16 [6, 128, 28672], P('grp', 'inp', 'out'), parts along dimension 0, may hold values from -6 to 6
- output_grads: bfloat16 [6, 128, 8192], P('grp', 'out', 'inp'), parts along dimension 0, may hold values from -6 to 6
- lengths: int32 [6], P('grp'), parts along dimension 0, may hold values from 1 to 128
- keep_mask: int32 [6, 128], P('grp'), parts along dimension 0, may hold values 0 or 1
- basis_in: bfloat16 [28672, 14336], P('out', 'inp'), may hold values from -0.03125 to 0.03125
- basis_out: bfloat16 [8192, 4096], P('inp', 'out'), may hold values from -0.0625 to 0.0625
Outputs:
- correction: float32 [8192, 14336], P(('grp', 'out'), 'inp'), parts along dimension 0
There are 2 independent parts, one for each index of `grp`. A program takes and returns all parts, laid end to end along the dimension named above; an argument that names none is the same for every part. Nothing has to cross between parts.
All inputs are finite; a program needn't handle non-finite values.
Results may differ from a plain program's by a relative error of at most 0.0043.
Values may be sent and summed in bfloat16 or wider, within the bound.
A program may use at most 192 MiB of HBM per device.

v0:
```python
import jax
import jax.numpy as jnp
from jax import lax
from jax.sharding import PartitionSpec as P


def shards(saved_inputs, output_grads, lengths, keep_mask, basis_in, basis_out):
    num_seqs = saved_inputs.shape[0]
    seq_slots = keep_mask.shape[1]
    rows_all = num_seqs * seq_slots
    positions = jnp.arange(seq_slots, dtype=jnp.int32)[None, :]
    valid_tokens = jnp.logical_and(
        positions < lengths[:, None], jnp.logical_or(keep_mask == 1, positions == 0)
    ).astype(jnp.float32)
    token_total = jnp.sum(valid_tokens)
    gathered_inputs = lax.all_gather(saved_inputs, "inp", axis=1, tiled=True)
    flat_inputs = gathered_inputs.reshape(rows_all, gathered_inputs.shape[2])
    partial_in = jnp.dot(flat_inputs, basis_in, preferred_element_type=jnp.float32)
    rotated_in = lax.psum(partial_in, "out").astype(jnp.bfloat16)
    rotated_in = rotated_in.reshape(num_seqs, seq_slots, basis_in.shape[1])
    gathered_grads = lax.all_gather(output_grads, "out", axis=1, tiled=True)
    flat_grads = gathered_grads.reshape(rows_all, gathered_grads.shape[2])
    partial_out = jnp.dot(flat_grads, basis_out, preferred_element_type=jnp.float32)
    grad_sums = lax.psum(partial_out, "inp")
    grad_sums = grad_sums.reshape(num_seqs, seq_slots, basis_out.shape[1])
    rotated_out = (grad_sums * valid_tokens[:, :, None]).astype(jnp.bfloat16)
    projected = jnp.einsum(
        "stg,sta->sga", rotated_out, rotated_in, preferred_element_type=jnp.float32
    )
    return jnp.sum(projected * projected, axis=0) / token_total


def solution(mesh):
    in_specs = (
        P("grp", "inp", "out"),
        P("grp", "out", "inp"),
        P("grp"),
        P("grp", None),
        P("out", "inp"),
        P("inp", "out"),
    )
    out_specs = P(("grp", "out"), "inp")
    return jax.shard_map(shards, mesh=mesh, in_specs=in_specs, out_specs=out_specs, check_vma=False)
```

profile of v0, /device:TPU:0, one launch (start us, length us, event | category | flops | bytes accessed | tf_op | source)
XLA Modules:
  0.0 347.0 jit_solution(3568730457348325207)
XLA Ops:
  6.5 0.0 all-gather.3.cloned.1.call-start
  6.5 0.7 all-gather.3.cloned.1.call-update
  7.3 0.0 all-gather.5.cloned.1.call-start
  7.3 0.7 all-gather.5.cloned.1.call-update
  8.0 0.0 all-reduce.3.cloned.1.call-start
  8.1 1.4 fusion.3
  9.4 39.3 %all-gather.3.cloned.1.call-done = bf16[3,128,2048]{2,1,0:T(8,128)(2,1)} async-done(((bf16[3,32,2048]{2,1,0:T(8,128)(2,1)}), bf16[3,128,2048]{2,1,0:T(8,128)(2,1)}) %all-gather.3.cloned.1.call-update) | async-done | bytes 1572880 | tf_op jit(solution)/shard_map/all_gather | solution.py:21
  48.8 4.5 %fusion.5 = f32[384,1024]{1,0:T(8,128)S(1)} fusion(bf16[384,2048]{1,0:T(8,128)(2,1)} %bitcast.12, bf16[2048,1024]{1,0:T(8,128)(2,1)} %param.11), kind=kOutput, calls=%fused_computation.9 | convolution fusion | flops 1610612736 | bytes 7340032 | tf_op jit(solution)/shard_map/dot_general | solution.py:23
  53.2 1.7 copy.7
  54.9 0.0 all-reduce.3.cloned.1.call-update
  54.9 36.2 %all-gather.5.cloned.1.call-done = bf16[3,128,7168]{2,1,0:T(8,128)(2,1)} async-done(((bf16[3,32,7168]{2,1,0:T(8,128)(2,1)}), bf16[3,128,7168]{2,1,0:T(8,128)(2,1)}) %all-gather.5.cloned.1.call-update) | async-done | bytes 5505040 | tf_op jit(solution)/shard_map/all_gather | solution.py:16
  91.1 30.8 %fusion.6 = f32[384,3584]{1,0:T(8,128)} fusion(bf16[384,7168]{1,0:T(8,128)(2,1)} %bitcast.11, bf16[7168,3584]{1,0:T(8,128)(2,1)} %param.10), kind=kOutput, calls=%fused_computation.10 | convolution fusion | flops 19730006016 | bytes 62390272 | tf_op jit(solution)/shard_map/dot_general | solution.py:18
  121.9 191.7 %all-reduce.4 = bf16[384,3584]{1,0:T(8,128)(2,1)S(1)} all-reduce(f32[384,3584]{1,0:T(8,128)} %fusion.6), channel_id=1, replica_groups=mesh['grp'=2,'inp'=4,'out'=4] {'out'}, use_global_device_ids=true, to_apply=%region_1.0 | all-reduce | flops 1376256 | bytes 8257536 | tf_op jit(solution)/shard_map/psum | solution.py:19
  313.6 0.0 all-reduce.3.cloned.1.call-done
  313.7 14.1 %multiply_reduce_fusion = f32[1024,3584]{1,0:T(8,128)} fusion(bf16[3,128,3584]{2,1,0:T(8,128)(2,1)S(1)} %bitcast.9, f32[3,128,1024]{1,2,0:T(8,128)} %all-reduce.3.cloned.1.call-done, f32[3,128]{1,0:T(4,128)S(1)} %get-tuple-element.6), kind=kOutput, calls=%fused_computation | convolution fusion | flops 2837708800 | bytes 19006976 | tf_op jit(solution)/shard_map/stg,sta->sga/dot_general | solution.py:27
  327.8 12.7 %broadcast_divide_fusion = f32[1024,3584]{1,0:T(8,128)} fusion(f32[1024,3584]{1,0:T(8,128)} %multiply_reduce_fusion, f32[]{:T(128)} %get-tuple-element.5), kind=kLoop, calls=%fused_computation.1 | loop fusion | flops 3670016 | bytes 29360132 | tf_op jit(solution)/shard_map/div | solution.py:30
  (1 shorter events, 0.0 us)
Async XLA Ops:
  6.5 42.2 %all-gather.3.cloned.1.call-start = ((), (), s32[]{:S(2)}) async-start(), calls=%async_computation | async-start | bytes 1966080 | tf_op jit(solution)/shard_map/all_gather | solution.py:21
  7.3 83.9 %all-gather.5.cloned.1.call-start = ((), (), s32[]{:S(2)}) async-start(), calls=%async_computation.2 | async-start | bytes 6881280 | tf_op jit(solution)/shard_map/all_gather | solution.py:16
  8.0 305.7 %all-reduce.3.cloned.1.call-start = ((), (), s32[]{:S(2)}) async-start(), calls=%async_computation.1 | async-start | bytes 3145728 | tf_op jit(solution)/shard_map/psum | solution.py:24
Sparse Core Ops, SparseCore 0:
  8.9 39.7 all-gather.2
  50.3 40.7 all-gather.4
  93.5 42.8 all-reduce.2
where the time goes:
time: 347 us
  blocking collectives  192 us (55%)
  waiting for transfers between devices  77 us (22%)
  matrix products  49.3 us (14%)
  other arithmetic  14.1 us (4%)
  between operations  13.1 us (4%)
    psum x1, blocking collectives, shards(): rotated_in = lax.psum(partial_in, 'out').astype(jnp.bfloat16)  192 us
    all_gather x1, waiting for transfers between devices, shards(): gathered_grads = lax.all_gather(output_grads, 'out', axis=1, tiled=True)  39.3 us
    all_gather x1, waiting for transfers between devices, shards(): gathered_inputs = lax.all_gather(saved_inputs, 'inp', axis=1, tiled=True)  36.2 us
    dot_general x1, matrix products, shards(): jnp.dot(flat_inputs, basis_in, preferred_element_type=jnp.float32)  30.8 us
    dot_general x1, matrix products, shards(): jnp.einsum('stg,sta->sga', rotated_out, rotated_in, preferred_element_typ...  14.1 us
    div x1, other arithmetic, shards(): return jnp.sum(projected * projected, axis=0) / token_total  12.7 us
  transfers between devices with their start and end apart: 3, of which 2 were waited for; matrix products, arithmetic and copies ran while one was open for 11% of the time, Pallas kernels for 0%

commit v1 on v0

v1 whole, which is shorter than its diff:
```python
import functools

import jax
import jax.numpy as jnp
from jax import lax
from jax.experimental import pallas as pl
from jax.experimental.pallas import tpu as pltpu
from jax.sharding import PartitionSpec as P

MESH = pl.DeviceIdType.MESH
F32 = jnp.float32
BF16 = jnp.bfloat16
WIDTH = 256
DEPTH = 3
LAG = 2


def rotate_kernel(n, x_ref, g_ref, valid_ref, win_ref, wout_ref, rin_ref, rout_ref,
                  xall, gall, part, from_left, from_right, to_right, to_left, wbuf, wout,
                  pout, csend, crecv, chip, xsend, xrecv, fown, frecv,
                  local_sem, w_sem, xs_sem, xr_sem, gs_sem, gr_sem, hs_sem, hr_sem,
                  rs_sem, rr_sem, ls_sem, lr_sem, os_sem, or_sem):
    num_seqs, slots = x_ref.shape[0], x_ref.shape[1]
    half_cols = chip.shape[1]
    pieces = part.shape[0]
    per_half = pieces // 2
    last = n - 1
    i = lax.axis_index("inp")
    k = lax.axis_index("out")
    xi, ci = lax.div(i, 2), lax.rem(i, 2)
    core = {"inp": xi * 2 + (1 - ci)}
    across = {"inp": (1 - xi) * 2 + ci}
    right = {"out": lax.rem(k + 1, n)}
    left = {"out": lax.rem(k + last, n)}

    def remote(src, dst, send, recv, to):
        return pltpu.make_async_remote_copy(src_ref=src, dst_ref=dst, send_sem=send, recv_sem=recv,
                                            device_id=to, device_id_type=MESH)

    def fetch(t):
        j = lax.rem(t, per_half)
        cols = pl.ds(pl.multiple_of(j * WIDTH, WIDTH), WIDTH)
        slot = lax.rem(t, DEPTH)
        return pltpu.make_async_copy(win_ref.at[:, cols], wbuf.at[slot], w_sem.at[slot])

    own_x = pltpu.make_async_copy(x_ref, xall.at[0, :, 0], local_sem.at[0])
    own_g = pltpu.make_async_copy(g_ref, gall.at[k], local_sem.at[1])
    own_w = pltpu.make_async_copy(wout_ref, wout, local_sem.at[2])
    own_x.start()
    own_g.start()
    own_w.start()
    for t in range(DEPTH - 1):
        fetch(jnp.int32(t)).start()

    barrier = pltpu.get_barrier_semaphore()
    pl.semaphore_signal(barrier, inc=1, device_id=core, device_id_type=MESH)
    pl.semaphore_signal(barrier, inc=1, device_id=across, device_id_type=MESH)

    @pl.when(k > 0)
    def _():
        pl.semaphore_signal(barrier, inc=1, device_id=left, device_id_type=MESH)

    @pl.when(k < last)
    def _():
        pl.semaphore_signal(barrier, inc=1, device_id=right, device_id_type=MESH)

    pl.semaphore_wait(barrier, 4 - jnp.where(k == 0, 1, 0) - jnp.where(k == last, 1, 0))

    x_across = remote(x_ref, xall.at[1, :, 0], xs_sem.at[0], xr_sem.at[0], across)
    x_core = remote(x_ref, xall.at[0, :, 1], xs_sem.at[1], xr_sem.at[1], core)
    x_hand = remote(xall.at[1, :, 0], xall.at[1, :, 1], xs_sem.at[2], xr_sem.at[2], core)
    x_across.start()
    x_core.start()

    def g_right(b):
        return remote(gall.at[b], gall.at[b], gs_sem.at[b], gr_sem.at[b], right)

    def g_left(b):
        return remote(gall.at[b], gall.at[b], hs_sem.at[b], hr_sem.at[b], left)

    own_g.wait()
    for h in range(n):
        lower, upper = k - h, k + h

        @pl.when(lower >= 0)
        def _():
            if h > 0:
                g_right(lower).wait_recv()

            @pl.when(k < last)
            def _():
                g_right(lower).start()

        @pl.when(upper <= last)
        def _():
            if h > 0:
                g_left(upper).wait_recv()

            @pl.when(k > 0)
            def _():
                g_left(upper).start()

    own_w.wait()
    rows = gall.shape[0] * gall.shape[1]
    grads = gall[...].reshape(rows, gall.shape[2])
    for h in range(2):
        pout[h] = jnp.dot(grads, wout[:, h * half_cols:(h + 1) * half_cols], preferred_element_type=F32)
    csend[...] = pout[1 - ci].astype(BF16)
    o_core = remote(csend, crecv, os_sem.at[0], or_sem.at[0], core)
    o_across = remote(xsend, xrecv, os_sem.at[1], or_sem.at[1], across)
    o_final = remote(fown, frecv, os_sem.at[2], or_sem.at[2], core)
    o_core.start()
    own_x.wait()
    x_core.wait_recv()

    def send_right(c):
        return remote(to_right.at[c], from_left.at[c], rs_sem.at[c], rr_sem.at[c], right)

    def send_left(c):
        return remote(to_left.at[c], from_right.at[c], ls_sem.at[c], lr_sem.at[c], left)

    far = jnp.maximum(k, last - k)

    def tick(t, carry):
        @pl.when(t == 2)
        def _():
            o_core.wait_recv()
            chip[...] = pout[ci] + crecv[...].astype(F32)
            xsend[...] = chip[...].astype(BF16)
            o_across.start()

        @pl.when(t == per_half - 4)
        def _():
            x_across.wait_recv()
            x_hand.start()

        @pl.when(t == per_half)
        def _():
            x_hand.wait_recv()

        @pl.when(t == per_half + 4)
        def _():
            o_across.wait_recv()
            fown[...] = ((chip[...] + xrecv[...].astype(F32)) * valid_ref[...]).astype(BF16)
            o_final.start()

        @pl.when(t < pieces)
        def _():
            fetch(t).wait()

            @pl.when(t + DEPTH - 1 < pieces)
            def _():
                fetch(t + DEPTH - 1).start()

            block = xall[lax.div(t, per_half)].reshape(num_seqs * 2 * slots, x_ref.shape[2])
            part[t] = jnp.dot(block, wbuf[lax.rem(t, DEPTH)], preferred_element_type=F32)

        c = t - LAG * k

        @pl.when((c >= 0) & (c < pieces))
        def _():
            @pl.when(k == 0)
            def _():
                to_right[c] = part[c].astype(BF16)

            @pl.when(k > 0)
            def _():
                send_right(c).wait_recv()

                @pl.when(k < last)
                def _():
                    to_right[c] = (part[c] + from_left[c].astype(F32)).astype(BF16)

            @pl.when(k < last)
            def _():
                send_right(c).start()

        d = t - LAG * (last - k)

        @pl.when((d >= 0) & (d < pieces))
        def _():
            @pl.when(k == last)
            def _():
                to_left[d] = part[d].astype(BF16)

            @pl.when(k < last)
            def _():
                send_left(d).wait_recv()

                @pl.when(k > 0)
                def _():
                    to_left[d] = (part[d] + from_right[d].astype(F32)).astype(BF16)

            @pl.when(k > 0)
            def _():
                send_left(d).start()

        e = t - LAG * far

        @pl.when((e >= 0) & (e < pieces))
        def _():
            h, j = lax.div(e, per_half), lax.rem(e, per_half)

            def put(total):
                total = total.astype(BF16)
                for s in range(num_seqs):
                    rin_ref[j, s, h] = total[s * 2 * slots:(s + 1) * 2 * slots]

            @pl.when(k == 0)
            def _():
                put(part[e] + from_right[e].astype(F32))

            @pl.when(k == last)
            def _():
                put(part[e] + from_left[e].astype(F32))

            @pl.when((k > 0) & (k < last))
            def _():
                put(part[e] + from_left[e].astype(F32) + from_right[e].astype(F32))

        return carry

    lax.fori_loop(0, pieces + LAG * last, tick, 0)

    def place(half, ref):
        for b in range(4):
            r = lax.rem(b // 2 + xi, 2) * 2 + lax.rem(b % 2 + ci, 2)
            for s in range(num_seqs):
                first = (b * num_seqs + s) * slots
                rout_ref[half, s, r] = ref[first:first + slots]

    place(ci, fown)
    o_final.wait_recv()
    place(1 - ci, frecv)

    for copy in (x_across, x_core, x_hand, o_core, o_across, o_final):
        copy.wait_send()
    for h in range(n):
        @pl.when((k - h >= 0) & (k < last))
        def _():
            g_right(k - h).wait_send()

        @pl.when((k + h <= last) & (k > 0))
        def _():
            g_left(k + h).wait_send()

    def drain(c, carry):
        @pl.when(k < last)
        def _():
            send_right(c).wait_send()

        @pl.when(k > 0)
        def _():
            send_left(c).wait_send()

        return carry

    lax.fori_loop(0, pieces, drain, 0)


def square_kernel(total_ref, rin_ref, rout_ref, out_ref, turned):
    num_seqs = turned.shape[0]
    rows, half_cols = rout_ref.shape[2] * rout_ref.shape[3], rout_ref.shape[4]

    @pl.when(pl.program_id(0) == 0)
    def _():
        for s in range(num_seqs):
            for h in range(2):
                block = rout_ref[h, s].reshape(rows, half_cols).astype(F32)
                turned[s, h * half_cols:(h + 1) * half_cols] = block.T.astype(BF16)

    total = total_ref[0, 0]
    step = half_cols // 2
    for m in range(turned.shape[1] // step):
        acc = None
        for s in range(num_seqs):
            proj = jnp.dot(turned[s, m * step:(m + 1) * step], rin_ref[0, s], preferred_element_type=F32)
            acc = proj * proj if acc is None else acc + proj * proj
        out_ref[m * step:(m + 1) * step] = acc / total


def token_mask(lengths, keep_mask):
    positions = jnp.arange(keep_mask.shape[1], dtype=jnp.int32)[None, :]
    return jnp.logical_and(
        positions < lengths[:, None], jnp.logical_or(keep_mask == 1, positions == 0)
    ).astype(F32)


def fused_shards(n, saved_inputs, output_grads, lengths, keep_mask, basis_in, basis_out):
    num_seqs, slots, feat = saved_inputs.shape
    gfeat = output_grads.shape[2]
    kin, kout = basis_in.shape[1], basis_out.shape[1]
    rows = num_seqs * slots * 4
    per_half = kin // WIDTH
    pieces = 2 * per_half
    half = rows // 2
    hc = kout // 2
    valid = token_mask(lengths, keep_mask)
    total = jnp.sum(valid).reshape(1, 1)
    column = valid.reshape(num_seqs, 4, slots).transpose(1, 0, 2).reshape(rows, 1)
    dma = pltpu.SemaphoreType.DMA
    anywhere = pl.BlockSpec(memory_space=pl.ANY)
    vmem = pl.BlockSpec(memory_space=pltpu.VMEM)
    rin, rout = pl.pallas_call(
        functools.partial(rotate_kernel, n),
        out_shape=(
            jax.ShapeDtypeStruct((per_half, num_seqs, 2, 2 * slots, WIDTH), BF16),
            jax.ShapeDtypeStruct((2, num_seqs, 4, slots, hc), BF16),
        ),
        in_specs=[anywhere, anywhere, vmem, anywhere, anywhere],
        out_specs=(vmem, vmem),
        scratch_shapes=[
            pltpu.VMEM((2, num_seqs, 2, slots, feat), BF16),
            pltpu.VMEM((n, num_seqs * slots, gfeat), BF16),
            pltpu.VMEM((pieces, half, WIDTH), F32),
            pltpu.VMEM((pieces, half, WIDTH), BF16),
            pltpu.VMEM((pieces, half, WIDTH), BF16),
            pltpu.VMEM((pieces, half, WIDTH), BF16),
            pltpu.VMEM((pieces, half, WIDTH), BF16),
            pltpu.VMEM((DEPTH, feat, WIDTH), BF16),
            pltpu.VMEM((gfeat, kout), BF16),
            pltpu.VMEM((2, rows, hc), F32),
            pltpu.VMEM((rows, hc), BF16),
            pltpu.VMEM((rows, hc), BF16),
            pltpu.VMEM((rows, hc), F32),
            pltpu.VMEM((rows, hc), BF16),
            pltpu.VMEM((rows, hc), BF16),
            pltpu.VMEM((rows, hc), BF16),
            pltpu.VMEM((rows, hc), BF16),
            dma((3,)), dma((DEPTH,)), dma((3,)), dma((3,)),
            dma((n,)), dma((n,)), dma((n,)), dma((n,)),
            dma((pieces,)), dma((pieces,)), dma((pieces,)), dma((pieces,)),
            dma((3,)), dma((3,)),
        ],
        compiler_params=pltpu.CompilerParams(
            collective_id=0, has_side_effects=True, vmem_limit_bytes=60 * 1024 * 1024
        ),
        cost_estimate=pl.CostEstimate(
            flops=2 * rows * (feat * kin + gfeat * kout), bytes_accessed=4 * feat * kin, transcendentals=0
        ),
        name="rotate",
    )(saved_inputs, output_grads.reshape(num_seqs * slots, gfeat), column, basis_in, basis_out)
    rin = rin.reshape(per_half, num_seqs, 4 * slots, WIDTH)
    return pl.pallas_call(
        square_kernel,
        grid=(per_half,),
        out_shape=jax.ShapeDtypeStruct((kout, kin), F32),
        in_specs=[
            pl.BlockSpec(memory_space=pltpu.SMEM),
            pl.BlockSpec((1, num_seqs, 4 * slots, WIDTH), lambda j: (j, 0, 0, 0)),
            pl.BlockSpec((2, num_seqs, 4, slots, hc), lambda j: (0, 0, 0, 0, 0)),
        ],
        out_specs=pl.BlockSpec((kout, WIDTH), lambda j: (0, j)),
        scratch_shapes=[pltpu.VMEM((num_seqs, kout, 4 * slots), BF16)],
        compiler_params=pltpu.CompilerParams(vmem_limit_bytes=32 * 1024 * 1024),
        cost_estimate=pl.CostEstimate(
            flops=2 * rows * kin * kout, bytes_accessed=4 * kin * kout, transcendentals=0
        ),
        name="square",
    )(total, rin, rout)


def plain_shards(saved_inputs, output_grads, lengths, keep_mask, basis_in, basis_out):
    num_seqs = saved_inputs.shape[0]
    seq_slots = keep_mask.shape[1]
    rows_all = num_seqs * seq_slots
    valid_tokens = token_mask(lengths, keep_mask)
    token_total = jnp.sum(valid_tokens)
    gathered_inputs = lax.all_gather(saved_inputs, "inp", axis=1, tiled=True)
    flat_inputs = gathered_inputs.reshape(rows_all, gathered_inputs.shape[2])
    partial_in = jnp.dot(flat_inputs, basis_in, preferred_element_type=F32)
    rotated_in = lax.psum(partial_in, "out").astype(BF16)
    rotated_in = rotated_in.reshape(num_seqs, seq_slots, basis_in.shape[1])
    gathered_grads = lax.all_gather(output_grads, "out", axis=1, tiled=True)
    flat_grads = gathered_grads.reshape(rows_all, gathered_grads.shape[2])
    partial_out = jnp.dot(flat_grads, basis_out, preferred_element_type=F32)
    grad_sums = lax.psum(partial_out, "inp")
    grad_sums = grad_sums.reshape(num_seqs, seq_slots, basis_out.shape[1])
    rotated_out = (grad_sums * valid_tokens[:, :, None]).astype(BF16)
    projected = jnp.einsum("stg,sta->sga", rotated_out, rotated_in, preferred_element_type=F32)
    return jnp.sum(projected * projected, axis=0) / token_total


def solution(mesh):
    in_specs = (
        P("grp", "inp", "out"),
        P("grp", "out", "inp"),
        P("grp"),
        P("grp", None),
        P("out", "inp"),
        P("inp", "out"),
    )
    out_specs = P(("grp", "out"), "inp")
    if mesh.shape["inp"] == 4 and mesh.shape["out"] == 4:
        body = functools.partial(fused_shards, mesh.shape["out"])
    else:
        body = plain_shards
    return jax.shard_map(body, mesh=mesh, in_specs=in_specs, out_specs=out_specs, check_vma=False)
```

time: 347 us -> 126 us (0.36)
  blocking collectives: 192 us -> 0 us
  Pallas kernels: 0 us -> 120 us
  waiting for transfers between devices: 77 us -> 0 us
  matrix products: 49.3 us -> 0 us
  between operations: 13.1 us -> 0.02 us
  other arithmetic: 14.1 us -> 1.33 us
    psum x1 -> x0, blocking collectives: 192 us -> none  [shards(): rotated_in = lax.psum(partial_in, 'out').astype(jnp.bfloat16)]
    pallas_call x0 -> x2, Pallas kernels: none -> 120 us  [the longest x1 108 us: fused_shards(): pl.pallas_call(functools.partial(rotate_kernel, n), out_shape=(jax.ShapeD...]
    all_gather x2 -> x0, waiting for transfers between devices: 75.5 us -> none  [the longest x1 39.3 us: shards(): gathered_grads = lax.all_gather(output_grads, 'out', axis=1, tiled=True)]
    dot_general x3 -> x0, matrix products: 49.3 us -> none  [the longest x1 30.8 us: shards(): jnp.dot(flat_inputs, basis_in, preferred_element_type=jnp.float32)]
    div x1 -> x0, other arithmetic: 12.7 us -> none  [shards(): return jnp.sum(projected * projected, axis=0) / token_total]
  transfers between devices with their start and end apart: 3 -> 0, of which waited for: 2 -> 0; matrix products, arithmetic and copies ran while one was open for 11% -> 0% of each run, Pallas kernels for 0% -> 0%
where the time goes in v1:
time: 126 us; the launch traced here: 125 us
  Pallas kernels  120 us (95%)
  local copies, waits for them, and re-layouts  3.88 us (3%)
  other arithmetic  1.33 us (1%)
    pallas_call x1, Pallas kernels, fused_shards(): pl.pallas_call(functools.partial(rotate_kernel, n), out_shape=(jax.ShapeD...  108 us
    pallas_call x1, Pallas kernels, fused_shards(): pl.pallas_call(square_kernel, grid=(per_half,), out_shape=jax.ShapeDtypeS...  12.1 us
    unnamed x4, local copies, waits for them, and re-layouts  2.9 us

profile of v1, /device:TPU:0, one launch (start us, length us, event | category | flops | bytes accessed | tf_op | source)
XLA Modules:
  0.0 125.4 jit_solution(2581173767515590833)
XLA Ops:
  0.0 1.3 %fusion.2 = (f32[]{:T(128)}, f32[3,128]{1,0:T(4,128)S(1)}) fusion(pred[128]{0:T(512)(128)(4,1)S(1)} %iota_compare_fusion.1, s32[3,128]{1,0:T(4,128)} %param.9, s32[3]{0:T(128)} %param.8), kind=kLoop, calls=%fused_computation.5 | loop fusion | flops 2303 | bytes 3216 | tf_op jit(solution)/shard_map/reduce_sum | solution.py:299
  1.3 0.1 reshape.23
  1.4 0.9 reshape.26.valid_ref
  2.3 108.1 %rotate.1 = (bf16[14,3,2,64,256]{4,3,2,1,0:T(8,128)(2,1)}, bf16[2,3,4,32,512]{4,3,2,1,0:T(8,128)(2,1)}) custom-call(bf16[3,32,7168]{2,1,0:T(8,128)(2,1)} %x_ref.1, bf16[96,2048]{1,0:T(8,128)(2,1)} %bitcast.8, f32[384,1]{1,0:T(8,128)} %reshape.26.valid_ref, bf16[7168,3584]{1,0:T(8,128)(2,1)} %win_ref.1, bf16[2048,1024]{1,0:T(8,128)(2,1)} %wout_ref.1), custom_call_target="tpu_custom_call" | custom-call | flops 21340618752 | bytes 102760448 | tf_op jit(solution)/shard_map/rotate/pallas_call | solution.py:304
  110.4 0.0 copy-start
  110.4 1.8 %copy-done = bf16[14,3,2,64,256]{4,3,2,1,0:T(8,128)(2,1)S(1)} copy-done((bf16[14,3,2,64,256]{4,3,2,1,0:T(8,128)(2,1)S(1)}, bf16[14,3,2,64,256]{4,3,2,1,0:T(8,128)(2,1)}, u32[]{:S(2)}) %copy-start) | copy-done | bytes 2752536
  112.2 0.0 copy-start.1
  112.2 1.1 copy-done.1
  113.3 12.1 %square.1 = f32[1024,3584]{1,0:T(8,128)} custom-call(f32[1,1]{1,0:T(1,128)} %bitcast.total_ref, bf16[14,3,128,256]{3,2,1,0:T(8,128)(2,1)S(1)} %bitcast.6, bf16[2,3,4,32,512]{4,3,2,1,0:T(8,128)(2,1)S(1)} %copy-done.1), custom_call_target="tpu_custom_call" | custom-call | flops 2818572288 | bytes 14680064 | tf_op jit(solution)/shard_map/square/pallas_call | solution.py:344
  (2 shorter events, 0.0 us)
Async XLA Ops:
  110.4 1.8 %copy-start = (bf16[14,3,2,64,256]{4,3,2,1,0:T(8,128)(2,1)S(1)}, bf16[14,3,2,64,256]{4,3,2,1,0:T(8,128)(2,1)}, u32[]{:S(2)}) copy-start(bf16[14,3,2,64,256]{4,3,2,1,0:T(8,128)(2,1)} %get-tuple-element.7) | copy-start | bytes 8257540
  112.2 1.1 copy-start.1

commit v2 on v1

--- a/solution.py
+++ b/solution.py
@@ -11,13 +11,14 @@
 F32 = jnp.float32
 BF16 = jnp.bfloat16
 WIDTH = 256
+HOP = 2
 DEPTH = 3
 LAG = 2
 
 
-def rotate_kernel(n, x_ref, g_ref, valid_ref, win_ref, wout_ref, rin_ref, rout_ref,
+def rotate_kernel(n, x_ref, g_ref, win_ref, wout_ref, rin_ref, rout_ref,
                   xall, gall, part, from_left, from_right, to_right, to_left, wbuf, wout,
-                  pout, csend, crecv, chip, xsend, xrecv, fown, frecv,
+                  pout, crecv, chip, xrecv, fown, frecv,
                   local_sem, w_sem, xs_sem, xr_sem, gs_sem, gr_sem, hs_sem, hr_sem,
                   rs_sem, rr_sem, ls_sem, lr_sem, os_sem, or_sem):
     num_seqs, slots = x_ref.shape[0], x_ref.shape[1]
@@ -43,7 +44,7 @@
         slot = lax.rem(t, DEPTH)
         return pltpu.make_async_copy(win_ref.at[:, cols], wbuf.at[slot], w_sem.at[slot])
 
-    own_x = pltpu.make_async_copy(x_ref, xall.at[0, :, 0], local_sem.at[0])
+    own_x = pltpu.make_async_copy(x_ref, xall.at[0, :, ci], local_sem.at[0])
     own_g = pltpu.make_async_copy(g_ref, gall.at[k], local_sem.at[1])
     own_w = pltpu.make_async_copy(wout_ref, wout, local_sem.at[2])
     own_x.start()
@@ -66,20 +67,16 @@
 
     pl.semaphore_wait(barrier, 4 - jnp.where(k == 0, 1, 0) - jnp.where(k == last, 1, 0))
 
-    x_across = remote(x_ref, xall.at[1, :, 0], xs_sem.at[0], xr_sem.at[0], across)
-    x_core = remote(x_ref, xall.at[0, :, 1], xs_sem.at[1], xr_sem.at[1], core)
-    x_hand = remote(xall.at[1, :, 0], xall.at[1, :, 1], xs_sem.at[2], xr_sem.at[2], core)
-    x_across.start()
-    x_core.start()
-
+    x_across = remote(x_ref, xall.at[1, :, ci], xs_sem.at[0], xr_sem.at[0], across)
+    x_core = remote(x_ref, xall.at[0, :, ci], xs_sem.at[1], xr_sem.at[1], core)
+    x_hand = remote(xall.at[1, :, ci], xall.at[1, :, ci], xs_sem.at[2], xr_sem.at[2], core)
     def g_right(b):
         return remote(gall.at[b], gall.at[b], gs_sem.at[b], gr_sem.at[b], right)
 
     def g_left(b):
         return remote(gall.at[b], gall.at[b], hs_sem.at[b], hr_sem.at[b], left)
 
-    own_g.wait()
-    for h in range(n):
+    def pass_grads(h):
         lower, upper = k - h, k + h
 
         @pl.when(lower >= 0)
@@ -100,16 +97,14 @@
             def _():
                 g_left(upper).start()
 
-    own_w.wait()
-    rows = gall.shape[0] * gall.shape[1]
-    grads = gall[...].reshape(rows, gall.shape[2])
-    for h in range(2):
-        pout[h] = jnp.dot(grads, wout[:, h * half_cols:(h + 1) * half_cols], preferred_element_type=F32)
-    csend[...] = pout[1 - ci].astype(BF16)
-    o_core = remote(csend, crecv, os_sem.at[0], or_sem.at[0], core)
-    o_across = remote(xsend, xrecv, os_sem.at[1], or_sem.at[1], across)
+    own_g.wait()
+    pass_grads(0)
+    x_core.start()
+    x_across.start()
+
+    o_core = remote(pout.at[1 - ci], crecv, os_sem.at[0], or_sem.at[0], core)
+    o_across = remote(chip, xrecv, os_sem.at[1], or_sem.at[1], across)
     o_final = remote(fown, frecv, os_sem.at[2], or_sem.at[2], core)
-    o_core.start()
     own_x.wait()
     x_core.wait_recv()
 
@@ -122,14 +117,26 @@
     far = jnp.maximum(k, last - k)
 
     def tick(t, carry):
-        @pl.when(t == 2)
+        for h in range(1, n):
+            @pl.when(t == HOP * h)
+            def _():
+                pass_grads(h)
+
+        @pl.when(t == HOP * n)
+        def _():
+            own_w.wait()
+            grads = gall[...].reshape(gall.shape[0] * gall.shape[1], gall.shape[2])
+            for h in range(2):
+                pout[h] = jnp.dot(grads, wout[:, h * half_cols:(h + 1) * half_cols], preferred_element_type=F32)
+            o_core.start()
+
+        @pl.when(t == HOP * n + 1)
         def _():
             o_core.wait_recv()
-            chip[...] = pout[ci] + crecv[...].astype(F32)
-            xsend[...] = chip[...].astype(BF16)
+            chip[...] = pout[ci] + crecv[...]
             o_across.start()
 
-        @pl.when(t == per_half - 4)
+        @pl.when(t == per_half - 3)
         def _():
             x_across.wait_recv()
             x_hand.start()
@@ -138,10 +145,10 @@
         def _():
             x_hand.wait_recv()
 
-        @pl.when(t == per_half + 4)
+        @pl.when(t == pieces - 1)
         def _():
             o_across.wait_recv()
-            fown[...] = ((chip[...] + xrecv[...].astype(F32)) * valid_ref[...]).astype(BF16)
+            fown[...] = (chip[...] + xrecv[...]).astype(BF16)
             o_final.start()
 
         @pl.when(t < pieces)
@@ -204,7 +211,7 @@
             def put(total):
                 total = total.astype(BF16)
                 for s in range(num_seqs):
-                    rin_ref[j, s, h] = total[s * 2 * slots:(s + 1) * 2 * slots]
+                    rin_ref[j, s, lax.rem(xi + h, 2)] = total[s * 2 * slots:(s + 1) * 2 * slots]
 
             @pl.when(k == 0)
             def _():
@@ -222,16 +229,9 @@
 
     lax.fori_loop(0, pieces + LAG * last, tick, 0)
 
-    def place(half, ref):
-        for b in range(4):
-            r = lax.rem(b // 2 + xi, 2) * 2 + lax.rem(b % 2 + ci, 2)
-            for s in range(num_seqs):
-                first = (b * num_seqs + s) * slots
-                rout_ref[half, s, r] = ref[first:first + slots]
-
-    place(ci, fown)
+    rout_ref[ci] = fown[...]
     o_final.wait_recv()
-    place(1 - ci, frecv)
+    rout_ref[1 - ci] = frecv[...]
 
     for copy in (x_across, x_core, x_hand, o_core, o_across, o_final):
         copy.wait_send()
@@ -258,25 +258,31 @@
     lax.fori_loop(0, pieces, drain, 0)
 
 
-def square_kernel(total_ref, rin_ref, rout_ref, out_ref, turned):
-    num_seqs = turned.shape[0]
-    rows, half_cols = rout_ref.shape[2] * rout_ref.shape[3], rout_ref.shape[4]
+def square_kernel(lengths_ref, keep_ref, rin_ref, rout_ref, out_ref, turned, scale):
+    num_seqs, _, seq_slots = turned.shape
+    half_cols = rout_ref.shape[4]
 
     @pl.when(pl.program_id(0) == 0)
     def _():
+        slot = lax.broadcasted_iota(jnp.int32, (1, seq_slots), 1)
+        total = jnp.float32(0)
         for s in range(num_seqs):
+            kept = (keep_ref[s:s + 1] == 1) | (slot == 0)
+            valid = jnp.where((slot < lengths_ref[s]) & kept, 1.0, 0.0).astype(F32)
+            total += jnp.sum(valid)
             for h in range(2):
-                block = rout_ref[h, s].reshape(rows, half_cols).astype(F32)
-                turned[s, h * half_cols:(h + 1) * half_cols] = block.T.astype(BF16)
-
-    total = total_ref[0, 0]
+                block = rout_ref[h, :, s].reshape(seq_slots, half_cols).astype(F32)
+                turned[s, h * half_cols:(h + 1) * half_cols] = (block.T * valid).astype(BF16)
+        scale[0] = total
+
+    share = 1.0 / jnp.full((1, out_ref.shape[1]), scale[0], F32)
     step = half_cols // 2
     for m in range(turned.shape[1] // step):
         acc = None
         for s in range(num_seqs):
             proj = jnp.dot(turned[s, m * step:(m + 1) * step], rin_ref[0, s], preferred_element_type=F32)
             acc = proj * proj if acc is None else acc + proj * proj
-        out_ref[m * step:(m + 1) * step] = acc / total
+        out_ref[m * step:(m + 1) * step] = acc * share
 
 
 def token_mask(lengths, keep_mask):
@@ -295,9 +301,6 @@
     pieces = 2 * per_half
     half = rows // 2
     hc = kout // 2
-    valid = token_mask(lengths, keep_mask)
-    total = jnp.sum(valid).reshape(1, 1)
-    column = valid.reshape(num_seqs, 4, slots).transpose(1, 0, 2).reshape(rows, 1)
     dma = pltpu.SemaphoreType.DMA
     anywhere = pl.BlockSpec(memory_space=pl.ANY)
     vmem = pl.BlockSpec(memory_space=pltpu.VMEM)
@@ -305,9 +308,9 @@
         functools.partial(rotate_kernel, n),
         out_shape=(
             jax.ShapeDtypeStruct((per_half, num_seqs, 2, 2 * slots, WIDTH), BF16),
-            jax.ShapeDtypeStruct((2, num_seqs, 4, slots, hc), BF16),
+            jax.ShapeDtypeStruct((2, rows, hc), BF16),
         ),
-        in_specs=[anywhere, anywhere, vmem, anywhere, anywhere],
+        in_specs=[anywhere] * 4,
         out_specs=(vmem, vmem),
         scratch_shapes=[
             pltpu.VMEM((2, num_seqs, 2, slots, feat), BF16),
@@ -320,11 +323,9 @@
             pltpu.VMEM((DEPTH, feat, WIDTH), BF16),
             pltpu.VMEM((gfeat, kout), BF16),
             pltpu.VMEM((2, rows, hc), F32),
-            pltpu.VMEM((rows, hc), BF16),
-            pltpu.VMEM((rows, hc), BF16),
             pltpu.VMEM((rows, hc), F32),
-            pltpu.VMEM((rows, hc), BF16),
-            pltpu.VMEM((rows, hc), BF16),
+            pltpu.VMEM((rows, hc), F32),
+            pltpu.VMEM((rows, hc), F32),
             pltpu.VMEM((rows, hc), BF16),
             pltpu.VMEM((rows, hc), BF16),
             dma((3,)), dma((DEPTH,)), dma((3,)), dma((3,)),
@@ -339,25 +340,27 @@
             flops=2 * rows * (feat * kin + gfeat * kout), bytes_accessed=4 * feat * kin, transcendentals=0
         ),
         name="rotate",
-    )(saved_inputs, output_grads.reshape(num_seqs * slots, gfeat), column, basis_in, basis_out)
+    )(saved_inputs, output_grads.reshape(num_seqs * slots, gfeat), basis_in, basis_out)
     rin = rin.reshape(per_half, num_seqs, 4 * slots, WIDTH)
+    rout = rout.reshape(2, 4, num_seqs, slots, hc)
     return pl.pallas_call(
         square_kernel,
         grid=(per_half,),
         out_shape=jax.ShapeDtypeStruct((kout, kin), F32),
         in_specs=[
             pl.BlockSpec(memory_space=pltpu.SMEM),
+            pl.BlockSpec((num_seqs, 4 * slots), lambda j: (0, 0)),
             pl.BlockSpec((1, num_seqs, 4 * slots, WIDTH), lambda j: (j, 0, 0, 0)),
-            pl.BlockSpec((2, num_seqs, 4, slots, hc), lambda j: (0, 0, 0, 0, 0)),
+            pl.BlockSpec((2, 4, num_seqs, slots, hc), lambda j: (0, 0, 0, 0, 0)),
         ],
         out_specs=pl.BlockSpec((kout, WIDTH), lambda j: (0, j)),
-        scratch_shapes=[pltpu.VMEM((num_seqs, kout, 4 * slots), BF16)],
-        compiler_params=pltpu.CompilerParams(vmem_limit_bytes=32 * 1024 * 1024),
+        scratch_shapes=[pltpu.VMEM((num_seqs, kout, 4 * slots), BF16), pltpu.SMEM((1,), F32)],
+        compiler_params=pltpu.CompilerParams(vmem_limit_bytes=60 * 1024 * 1024),
         cost_estimate=pl.CostEstimate(
             flops=2 * rows * kin * kout, bytes_accessed=4 * kin * kout, transcendentals=0
         ),
         name="square",
-    )(total, rin, rout)
+    )(lengths, keep_mask, rin, rout)
 
 
 def plain_shards(saved_inputs, output_grads, lengths, keep_mask, basis_in, basis_out):

time: 126 us -> 115 us (0.913)
  Pallas kernels: 120 us -> 114 us
  local copies, waits for them, and re-layouts: 3.88 us -> 0 us
  other arithmetic: 1.33 us -> 0 us
    pallas_call x1, Pallas kernels: 108 us -> 99.6 us  [fused_shards(): pl.pallas_call(functools.partial(rotate_kernel, n), out_shape=(jax.ShapeD...]
    unnamed x4 -> x0, local copies, waits for them, and re-layouts: 2.9 us -> none
    pallas_call x1, Pallas kernels: 12.1 us -> 14.8 us  [fused_shards(): pl.pallas_call(square_kernel, grid=(per_half,), out_shape=jax.ShapeDtypeS...]
    reduce_sum x1 -> x0, other arithmetic: 1.32 us -> none  [fused_shards(): total = jnp.sum(valid).reshape(1, 1)]
where the time goes in v2:
time: 115 us; the launch traced here: 114 us
  Pallas kernels  114 us (99%)
    pallas_call x1, Pallas kernels, fused_shards(): pl.pallas_call(functools.partial(rotate_kernel, n), out_shape=(jax.ShapeD...  99.6 us
    pallas_call x1, Pallas kernels, fused_shards(): pl.pallas_call(square_kernel, grid=(per_half,), out_shape=jax.ShapeDtypeS...  14.8 us

profile of v2, /device:TPU:0, one launch (start us, length us, event | category | flops | bytes accessed | tf_op | source)
XLA Modules:
  0.0 114.4 jit_solution(11852636228278947998)
XLA Ops:
  0.0 99.6 %rotate.1 = (bf16[14,3,2,64,256]{4,3,2,1,0:T(8,128)(2,1)}, bf16[2,384,512]{2,1,0:T(8,128)(2,1)}) custom-call(bf16[3,32,7168]{2,1,0:T(8,128)(2,1)} %x_ref.1, bf16[96,2048]{1,0:T(8,128)(2,1)} %bitcast.5, bf16[7168,3584]{1,0:T(8,128)(2,1)} %win_ref.1, bf16[2048,1024]{1,0:T(8,128)(2,1)} %wout_ref.1), custom_call_target="tpu_custom_call" | custom-call | flops 21340618752 | bytes 102760448 | tf_op jit(solution)/shard_map/rotate/pallas_call | solution.py:307
  99.6 14.8 %square.1 = f32[1024,3584]{1,0:T(8,128)} custom-call(s32[3]{0:T(128)} %lengths_ref.1, s32[3,128]{1,0:T(4,128)} %keep_ref.1, bf16[14,3,128,256]{3,2,1,0:T(8,128)(2,1)} %bitcast.3, bf16[2,4,3,32,512]{4,3,2,1,0:T(8,128)(2,1)} %bitcast.4), custom_call_target="tpu_custom_call" | custom-call | flops 2818572288 | bytes 14680064 | tf_op jit(solution)/shard_map/square/pallas_call | solution.py:346

commit v3 on v2

--- a/solution.py
+++ b/solution.py
@@ -97,10 +97,10 @@
             def _():
                 g_left(upper).start()
 
+    x_across.start()
     own_g.wait()
     pass_grads(0)
     x_core.start()
-    x_across.start()
 
     o_core = remote(pout.at[1 - ci], crecv, os_sem.at[0], or_sem.at[0], core)
     o_across = remote(chip, xrecv, os_sem.at[1], or_sem.at[1], across)
@@ -134,12 +134,12 @@
         def _():
             o_core.wait_recv()
             chip[...] = pout[ci] + crecv[...]
-            o_across.start()
-
-        @pl.when(t == per_half - 3)
+
+        @pl.when(t == per_half - 2)
         def _():
             x_across.wait_recv()
             x_hand.start()
+            o_across.start()
 
         @pl.when(t == per_half)
         def _():
@@ -275,14 +275,16 @@
                 turned[s, h * half_cols:(h + 1) * half_cols] = (block.T * valid).astype(BF16)
         scale[0] = total
 
-    share = 1.0 / jnp.full((1, out_ref.shape[1]), scale[0], F32)
+    share = 1.0 / jnp.full((1, rin_ref.shape[3]), scale[0], F32)
     step = half_cols // 2
-    for m in range(turned.shape[1] // step):
-        acc = None
-        for s in range(num_seqs):
-            proj = jnp.dot(turned[s, m * step:(m + 1) * step], rin_ref[0, s], preferred_element_type=F32)
-            acc = proj * proj if acc is None else acc + proj * proj
-        out_ref[m * step:(m + 1) * step] = acc * share
+    for q in range(rin_ref.shape[0]):
+        wide = rin_ref.shape[3]
+        for m in range(turned.shape[1] // step):
+            acc = None
+            for s in range(num_seqs):
+                proj = jnp.dot(turned[s, m * step:(m + 1) * step], rin_ref[q, s], preferred_element_type=F32)
+                acc = proj * proj if acc is None else acc + proj * proj
+            out_ref[m * step:(m + 1) * step, q * wide:(q + 1) * wide] = acc * share
 
 
 def token_mask(lengths, keep_mask):
@@ -345,15 +347,15 @@
     rout = rout.reshape(2, 4, num_seqs, slots, hc)
     return pl.pallas_call(
         square_kernel,
-        grid=(per_half,),
+        grid=(per_half // 2,),
         out_shape=jax.ShapeDtypeStruct((kout, kin), F32),
         in_specs=[
             pl.BlockSpec(memory_space=pltpu.SMEM),
             pl.BlockSpec((num_seqs, 4 * slots), lambda j: (0, 0)),
-            pl.BlockSpec((1, num_seqs, 4 * slots, WIDTH), lambda j: (j, 0, 0, 0)),
+            pl.BlockSpec((2, num_seqs, 4 * slots, WIDTH), lambda j: (j, 0, 0, 0)),
             pl.BlockSpec((2, 4, num_seqs, slots, hc), lambda j: (0, 0, 0, 0, 0)),
         ],
-        out_specs=pl.BlockSpec((kout, WIDTH), lambda j: (0, j)),
+        out_specs=pl.BlockSpec((kout, 2 * WIDTH), lambda j: (0, j)),
         scratch_shapes=[pltpu.VMEM((num_seqs, kout, 4 * slots), BF16), pltpu.SMEM((1,), F32)],
         compiler_params=pltpu.CompilerParams(vmem_limit_bytes=60 * 1024 * 1024),
         cost_estimate=pl.CostEstimate(

time: 115 us -> 111 us (0.965)
  Pallas kernels: 114 us -> 111 us
    pallas_call x1, Pallas kernels: 14.8 us -> 11.1 us  [fused_shards(): pl.pallas_call(square_kernel, grid=(per_half // 2,), out_shape=jax.ShapeD...]
where the time goes in v3:
time: 111 us
  Pallas kernels  111 us (100%)
    pallas_call x1, Pallas kernels, fused_shards(): pl.pallas_call(functools.partial(rotate_kernel, n), out_shape=(jax.ShapeD...  99.6 us
    pallas_call x1, Pallas kernels, fused_shards(): pl.pallas_call(square_kernel, grid=(per_half // 2,), out_shape=jax.ShapeD...  11.1 us

profile of v3, /device:TPU:0, one launch (start us, length us, event | category | flops | bytes accessed | tf_op | source)
XLA Modules:
  0.0 110.7 jit_solution(9695095131670965766)
XLA Ops:
  0.0 99.6 %rotate.1 = (bf16[14,3,2,64,256]{4,3,2,1,0:T(8,128)(2,1)}, bf16[2,384,512]{2,1,0:T(8,128)(2,1)}) custom-call(bf16[3,32,7168]{2,1,0:T(8,128)(2,1)} %x_ref.1, bf16[96,2048]{1,0:T(8,128)(2,1)} %bitcast.5, bf16[7168,3584]{1,0:T(8,128)(2,1)} %win_ref.1, bf16[2048,1024]{1,0:T(8,128)(2,1)} %wout_ref.1), custom_call_target="tpu_custom_call" | custom-call | flops 21340618752 | bytes 102760448 | tf_op jit(solution)/shard_map/rotate/pallas_call | solution.py:309
  99.6 11.1 %square.1 = f32[1024,3584]{1,0:T(8,128)} custom-call(s32[3]{0:T(128)} %lengths_ref.1, s32[3,128]{1,0:T(4,128)} %keep_ref.1, bf16[14,3,128,256]{3,2,1,0:T(8,128)(2,1)} %bitcast.3, bf16[2,4,3,32,512]{4,3,2,1,0:T(8,128)(2,1)} %bitcast.4), custom_call_target="tpu_custom_call" | custom-call | flops 2818572288 | bytes 14680064 | tf_op jit(solution)/shard_map/square/pallas_call | solution.py:348
